TPU v7x, 32 devices: a whole 2x2x4 slice. The times are simulated.
32 devices in a mesh: groups: 1, row: 4 (over x, core), col: 8 (over z, y).
Axes of the slice: x: 2, y: 2, z: 4, core: 2. Of those that a mesh axis runs over, the one named last changes fastest.
Arguments:
- a_tiles: bfloat16 [128, 27, 128, 128], P(('groups', 'row', 'col')), may hold values from -0.5 to 0.5
- a_cols: int32 [128, 27], P(('groups', 'row', 'col')), may hold values from 0 to 127, as said below
- p_tiles: bfloat16 [128, 4, 128, 128], P(('groups', 'row', 'col')), may hold values from -0.5 to 0.5
- p_cols: int32 [128, 4], P('groups'), may hold values from 0 to 15, as said below
Outputs:
- coarse: float32 [2048, 1536], P(('groups', 'row', 'col'))
Inputs may be any that keep to these rules, and one draw needn't show every extreme that they name: `a_cols`: in each row i the 27 columns are distinct, include i itself, and each equals (i + d) mod 128 for some d with |d| <= 16. `p_cols`: in each row i the 4 columns are distinct, include the row's aggregate (i // 32) * 4 + (i % 32) // 8, and all lie in the coarse blocks of the row's own grid row, (i // 32) * 4 to (i // 32) * 4 + 3.
All inputs are finite; a program needn't handle non-finite values.
Results may differ from a plain program's by a relative error of at most 0.008.
Values may be sent and summed in bfloat16 or wider, within the bound.
A program may use at most 128 MiB of HBM per device.

v0:
```python
import jax
import jax.numpy as jnp
from jax import lax
from jax.sharding import PartitionSpec as P

AGG = 8


def extended_2(value, sides, width):
    for axis, dim in sides:
        count, length = (lax.axis_size(axis), value.shape[dim])
        up = [(i, (i + 1) % count) for i in range(count)]
        down = [(j, i) for i, j in up]
        last = lax.slice_in_dim(value, length - width, length, axis=dim)
        initial = lax.slice_in_dim(value, 0, width, axis=dim)
        before = lax.ppermute(last, axis, up)
        after = lax.ppermute(initial, axis, down)
        value = jnp.concatenate([before, value, after], axis=dim)
    return value


def local(a_tiles, a_cols, p_tiles, p_cols):
    rows_dev = a_tiles.shape[0]
    tile_size = a_tiles.shape[2]
    col_count = lax.axis_size("col")
    row_count = lax.axis_size("row")
    slab_len = rows_dev * col_count
    reach = slab_len // 2
    total_rows = slab_len * row_count
    coarse_slab = slab_len // AGG
    window = 3 * coarse_slab
    band_cols = coarse_slab * tile_size
    row_index = lax.axis_index("row")
    col_index = lax.axis_index("col")
    slab_tiles = lax.all_gather(p_tiles, "col", axis=0, tiled=True)
    extended = extended_2(slab_tiles, (("row", 0),), reach)
    ext_pos = jnp.arange(slab_len + 2 * reach, dtype=jnp.int32)
    ext_rows = (row_index * slab_len - reach + ext_pos) % total_rows
    ext_cols = jnp.take(p_cols, ext_rows, axis=0)
    band_index = (ext_pos >= reach).astype(jnp.int32) + (ext_pos >= reach + slab_len).astype(
        jnp.int32
    )
    ext_window = band_index[:, None] * coarse_slab + ext_cols % coarse_slab
    first_row = (row_index * col_count + col_index) * rows_dev
    own_cols = lax.dynamic_slice_in_dim(p_cols, first_row, rows_dev, 0)
    local_ids = own_cols % coarse_slab
    col_pos = (a_cols - row_index * slab_len + reach) % total_rows
    window_ids = jnp.arange(window, dtype=jnp.int32)
    owner_ids = jnp.arange(coarse_slab, dtype=jnp.int32)

    def row_product(carry, row_items):
        a_row_tiles, row_pos = row_items
        picked = jnp.take(extended, row_pos, axis=0)
        products = jnp.einsum(
            "jab,jqbc->jqac", a_row_tiles, picked, preferred_element_type=jnp.float32
        )
        window_marks = (jnp.take(ext_window, row_pos, axis=0)[:, :, None] == window_ids).astype(
            jnp.bfloat16
        )
        upper_half = products.astype(jnp.bfloat16)
        lower_half = (products - upper_half.astype(jnp.float32)).astype(jnp.bfloat16)
        merged = jnp.einsum(
            "jqw,jqac->awc", window_marks, upper_half, preferred_element_type=jnp.float32
        )
        merged = merged + jnp.einsum(
            "jqw,jqac->awc", window_marks, lower_half, preferred_element_type=jnp.float32
        )
        return (carry, merged.reshape(tile_size, window * tile_size).astype(jnp.bfloat16))

    _, ap_rows = lax.scan(row_product, jnp.zeros((), jnp.float32), (a_tiles, col_pos))
    owner_marks = (local_ids[:, :, None] == owner_ids).astype(jnp.bfloat16)
    placed = jnp.einsum("iqm,iqba->ibma", owner_marks, p_tiles, preferred_element_type=jnp.float32)
    placed = placed.astype(jnp.bfloat16).reshape(rows_dev * tile_size, band_cols)
    ap_flat = ap_rows.reshape(rows_dev * tile_size, window * tile_size)
    partial_value = jnp.einsum("km,kn->mn", placed, ap_flat, preferred_element_type=jnp.float32)
    return lax.psum_scatter(partial_value, "col", scatter_dimension=0, tiled=True)


def solution(mesh):
    in_specs = (
        P(("groups", "row", "col"), None, None, None),
        P(("groups", "row", "col"), None),
        P(("groups", "row", "col"), None, None, None),
        P("groups", None),
    )
    out_specs = P(("groups", "row", "col"), None)
    return jax.shard_map(local, mesh=mesh, in_specs=in_specs, out_specs=out_specs, check_vma=False)
```

profile of v0, /device:TPU:1, one launch (start us, length us, event | category | flops | bytes accessed | tf_op | source)
XLA Modules:
  0.0 372.8 jit_solution(16727027814076135330)
XLA Ops:
  7.3 76.5 %all-gather.2.cloned.1.call-done = bf16[32,4,128,128]{3,2,1,0:T(8,128)(2,1)} async-done(((bf16[4,4,128,128]{3,2,1,0:T(8,128)(2,1)}), bf16[32,4,128,128]{3,2,1,0:T(8,128)(2,1)}) %all-gather.2.cloned.1.call-update) | async-done | bytes 4194320 | tf_op jit(solution)/shard_map/all_gather | solution.py:35
  83.8 4.0 %fusion.36 = (bf16[16,4,128,128]{3,2,1,0:T(8,128)(2,1)}, bf16[16,4,128,128]{3,2,1,0:T(8,128)(2,1)S(1)}) fusion(bf16[32,4,128,128]{3,2,1,0:T(8,128)(2,1)} %all-gather.2.cloned.1.call-done), kind=kLoop, calls=%fused_computation.71 | loop fusion | bytes 8388608 | tf_op jit(solution)/shard_map/slice | solution.py:14
  87.8 2.9 collective-permute-start
  93.7 42.2 %collective-permute-done = bf16[16,4,128,128]{3,2,1,0:T(8,128)(2,1)} collective-permute-done((bf16[16,4,128,128]{3,2,1,0:T(8,128)(2,1)}, bf16[16,4,128,128]{3,2,1,0:T(8,128)(2,1)}, u32[]{:S(2)}, u32[]{:S(2)}) %collective-permute-start) | collective-permute-done | bytes 2097184 | tf_op jit(solution)/shard_map/ppermute | solution.py:16
  137.2 7.2 %pad_maximum_fusion = bf16[64,4,128,128]{3,2,1,0:T(8,128)(2,1)} fusion(bf16[16,4,128,128]{3,2,1,0:T(8,128)(2,1)} %collective-permute-done.1, bf16[32,4,128,128]{3,2,1,0:T(8,128)(2,1)} %all-gather.2.cloned.1.call-done, bf16[16,4,128,128]{3,2,1,0:T(8,128)(2,1)} %collective-permute-done), kind=kLoop, calls=%fused_computation.32 | loop fusion | flops 8388608 | bytes 16777216 | tf_op jit(solution)/shard_map/concatenate | solution.py:18
  144.4 145.6 %while.11 = (s32[]{:T(128)}, bf16[4,128,1536]{2,1,0:T(8,128)(2,1)}, s32[4,27]{1,0:T(4,128)S(1)}, bf16[64,4,128,128]{3,2,1,0:T(8,128)(2,1)}, bf16[4,27,128,128]{3...) while((s32[]{:T(128)}, bf16[4,128,1536]{2,1,0:T(8,128)(2,1)}, s32[4,27]{1,0:T(4,128)S(1)}, ...), condition=%wide.region_1.2_spmd.clone, body=%wide.region_0.1_spmd.clone.sunk | while | flops 547164032 | bytes 58323752 | solution.py:70
  144.5 4.6 %gather_fusion = bf16[27,4,128,128]{3,2,1,0:T(8,128)(2,1)S(1)} fusion(bf16[64,4,128,128]{3,2,1,0:T(8,128)(2,1)} %get-tuple-element.131, s32[1024]{0:T(1024)S(1)} %pad_clamp_fusion.3), kind=kCustom, calls=%fused_computation.clone.clone.1 | custom fusion | bytes 7077996 | tf_op jit(solution)/shard_map/while/body/eval_jaxpr/jit(_take)/gather | solution.py:53
  149.1 5.8 %fusion.52 = (bf16[27,4,128,128]{2,3,1,0:T(8,128)(2,1)}, bf16[27,4,128,128]{2,3,1,0:T(8,128)(2,1)}) fusion(bf16[4,27,128,128]{3,2,1,0:T(8,128)(2,1)} %get-tuple-element.132, s32[]{:T(128)} %get-tuple-element.121, bf16[27,4,128,128]{3,2,1,0:T(8,128)(2,1)S(1)} %gather_fusion, pred[27]{0:T(512)(128)(4,1)S(1)} %compare_and_fusion.3), kind=kOutput, calls=%fused_computation.6.clone.1 | convolution fusion | flops 461832192 | bytes 11502107 | tf_op jit(solution)/shard_map/while/body/eval_jaxpr/jab,jqbc->jqac/dot_general | solution.py:54
  154.9 7.8 %copy.57 = bf16[27,4,128,128]{3,0,1,2:T(8,128)(2,1)} copy(bf16[27,4,128,128]{2,3,1,0:T(8,128)(2,1)} %get-tuple-element.112) | data formatting | bytes 7077888 | tf_op jit(solution)/shard_map/while/body/eval_jaxpr/convert_element_type | solution.py:61
  166.5 3.9 %convolution_bitcast_fusion.3 = f32[128,128,12]{1,2,0:T(8,128)} fusion(bf16[27,4,128,128]{3,0,1,2:T(8,128)(2,1)} %copy.57, s32[27,4]{0,1:T(4,128)S(1)} %copy.58), kind=kOutput, calls=%fused_computation.11.clone.1 | convolution fusion | flops 42468624 | bytes 4325808 | tf_op jit(solution)/shard_map/while/body/eval_jaxpr/jqw,jqac->awc/dot_general | solution.py:65
  170.4 5.9 %copy.59 = bf16[27,4,128,128]{3,0,1,2:T(8,128)(2,1)} copy(bf16[27,4,128,128]{2,3,1,0:T(8,128)(2,1)S(1)} %copy-done) | data formatting | bytes 7077888 | tf_op jit(solution)/shard_map/while/body/eval_jaxpr/convert_element_type | solution.py:60
  176.3 3.2 fusion.53
  180.9 4.6 %gather_fusion = bf16[27,4,128,128]{3,2,1,0:T(8,128)(2,1)S(1)} fusion(bf16[64,4,128,128]{3,2,1,0:T(8,128)(2,1)} %get-tuple-element.131, s32[1024]{0:T(1024)S(1)} %pad_clamp_fusion.3), kind=kCustom, calls=%fused_computation.clone.clone.1 | custom fusion | bytes 7077996 | tf_op jit(solution)/shard_map/while/body/eval_jaxpr/jit(_take)/gather | solution.py:53
  185.5 5.8 %fusion.52 = (bf16[27,4,128,128]{2,3,1,0:T(8,128)(2,1)}, bf16[27,4,128,128]{2,3,1,0:T(8,128)(2,1)}) fusion(bf16[4,27,128,128]{3,2,1,0:T(8,128)(2,1)} %get-tuple-element.132, s32[]{:T(128)} %get-tuple-element.121, bf16[27,4,128,128]{3,2,1,0:T(8,128)(2,1)S(1)} %gather_fusion, pred[27]{0:T(512)(128)(4,1)S(1)} %compare_and_fusion.3), kind=kOutput, calls=%fused_computation.6.clone.1 | convolution fusion | flops 461832192 | bytes 11502107 | tf_op jit(solution)/shard_map/while/body/eval_jaxpr/jab,jqbc->jqac/dot_general | solution.py:54
  191.3 7.8 %copy.57 = bf16[27,4,128,128]{3,0,1,2:T(8,128)(2,1)} copy(bf16[27,4,128,128]{2,3,1,0:T(8,128)(2,1)} %get-tuple-element.112) | data formatting | bytes 7077888 | tf_op jit(solution)/shard_map/while/body/eval_jaxpr/convert_element_type | solution.py:61
  202.9 3.9 %convolution_bitcast_fusion.3 = f32[128,128,12]{1,2,0:T(8,128)} fusion(bf16[27,4,128,128]{3,0,1,2:T(8,128)(2,1)} %copy.57, s32[27,4]{0,1:T(4,128)S(1)} %copy.58), kind=kOutput, calls=%fused_computation.11.clone.1 | convolution fusion | flops 42468624 | bytes 4325808 | tf_op jit(solution)/shard_map/while/body/eval_jaxpr/jqw,jqac->awc/dot_general | solution.py:65
  206.8 5.9 %copy.59 = bf16[27,4,128,128]{3,0,1,2:T(8,128)(2,1)} copy(bf16[27,4,128,128]{2,3,1,0:T(8,128)(2,1)S(1)} %copy-done) | data formatting | bytes 7077888 | tf_op jit(solution)/shard_map/while/body/eval_jaxpr/convert_element_type | solution.py:60
  212.7 3.2 fusion.53
  217.3 4.6 %gather_fusion = bf16[27,4,128,128]{3,2,1,0:T(8,128)(2,1)S(1)} fusion(bf16[64,4,128,128]{3,2,1,0:T(8,128)(2,1)} %get-tuple-element.131, s32[1024]{0:T(1024)S(1)} %pad_clamp_fusion.3), kind=kCustom, calls=%fused_computation.clone.clone.1 | custom fusion | bytes 7077996 | tf_op jit(solution)/shard_map/while/body/eval_jaxpr/jit(_take)/gather | solution.py:53
  221.9 5.8 %fusion.52 = (bf16[27,4,128,128]{2,3,1,0:T(8,128)(2,1)}, bf16[27,4,128,128]{2,3,1,0:T(8,128)(2,1)}) fusion(bf16[4,27,128,128]{3,2,1,0:T(8,128)(2,1)} %get-tuple-element.132, s32[]{:T(128)} %get-tuple-element.121, bf16[27,4,128,128]{3,2,1,0:T(8,128)(2,1)S(1)} %gather_fusion, pred[27]{0:T(512)(128)(4,1)S(1)} %compare_and_fusion.3), kind=kOutput, calls=%fused_computation.6.clone.1 | convolution fusion | flops 461832192 | bytes 11502107 | tf_op jit(solution)/shard_map/while/body/eval_jaxpr/jab,jqbc->jqac/dot_general | solution.py:54
  227.7 7.8 %copy.57 = bf16[27,4,128,128]{3,0,1,2:T(8,128)(2,1)} copy(bf16[27,4,128,128]{2,3,1,0:T(8,128)(2,1)} %get-tuple-element.112) | data formatting | bytes 7077888 | tf_op jit(solution)/shard_map/while/body/eval_jaxpr/convert_element_type | solution.py:61
  239.3 3.9 %convolution_bitcast_fusion.3 = f32[128,128,12]{1,2,0:T(8,128)} fusion(bf16[27,4,128,128]{3,0,1,2:T(8,128)(2,1)} %copy.57, s32[27,4]{0,1:T(4,128)S(1)} %copy.58), kind=kOutput, calls=%fused_computation.11.clone.1 | convolution fusion | flops 42468624 | bytes 4325808 | tf_op jit(solution)/shard_map/while/body/eval_jaxpr/jqw,jqac->awc/dot_general | solution.py:65
  243.2 5.9 %copy.59 = bf16[27,4,128,128]{3,0,1,2:T(8,128)(2,1)} copy(bf16[27,4,128,128]{2,3,1,0:T(8,128)(2,1)S(1)} %copy-done) | data formatting | bytes 7077888 | tf_op jit(solution)/shard_map/while/body/eval_jaxpr/convert_element_type | solution.py:60
  249.1 3.2 fusion.53
  253.7 4.6 %gather_fusion = bf16[27,4,128,128]{3,2,1,0:T(8,128)(2,1)S(1)} fusion(bf16[64,4,128,128]{3,2,1,0:T(8,128)(2,1)} %get-tuple-element.131, s32[1024]{0:T(1024)S(1)} %pad_clamp_fusion.3), kind=kCustom, calls=%fused_computation.clone.clone.1 | custom fusion | bytes 7077996 | tf_op jit(solution)/shard_map/while/body/eval_jaxpr/jit(_take)/gather | solution.py:53
  258.3 5.8 %fusion.52 = (bf16[27,4,128,128]{2,3,1,0:T(8,128)(2,1)}, bf16[27,4,128,128]{2,3,1,0:T(8,128)(2,1)}) fusion(bf16[4,27,128,128]{3,2,1,0:T(8,128)(2,1)} %get-tuple-element.132, s32[]{:T(128)} %get-tuple-element.121, bf16[27,4,128,128]{3,2,1,0:T(8,128)(2,1)S(1)} %gather_fusion, pred[27]{0:T(512)(128)(4,1)S(1)} %compare_and_fusion.3), kind=kOutput, calls=%fused_computation.6.clone.1 | convolution fusion | flops 461832192 | bytes 11502107 | tf_op jit(solution)/shard_map/while/body/eval_jaxpr/jab,jqbc->jqac/dot_general | solution.py:54
  264.1 7.8 %copy.57 = bf16[27,4,128,128]{3,0,1,2:T(8,128)(2,1)} copy(bf16[27,4,128,128]{2,3,1,0:T(8,128)(2,1)} %get-tuple-element.112) | data formatting | bytes 7077888 | tf_op jit(solution)/shard_map/while/body/eval_jaxpr/convert_element_type | solution.py:61
  275.7 3.9 %convolution_bitcast_fusion.3 = f32[128,128,12]{1,2,0:T(8,128)} fusion(bf16[27,4,128,128]{3,0,1,2:T(8,128)(2,1)} %copy.57, s32[27,4]{0,1:T(4,128)S(1)} %copy.58), kind=kOutput, calls=%fused_computation.11.clone.1 | convolution fusion | flops 42468624 | bytes 4325808 | tf_op jit(solution)/shard_map/while/body/eval_jaxpr/jqw,jqac->awc/dot_general | solution.py:65
  279.6 5.9 %copy.59 = bf16[27,4,128,128]{3,0,1,2:T(8,128)(2,1)} copy(bf16[27,4,128,128]{2,3,1,0:T(8,128)(2,1)S(1)} %copy-done) | data formatting | bytes 7077888 | tf_op jit(solution)/shard_map/while/body/eval_jaxpr/convert_element_type | solution.py:60
  285.5 3.2 fusion.53
  290.0 4.2 %fusion.20 = f32[512,1536]{1,0:T(8,128)} fusion(bf16[512,1536]{1,0:T(8,128)(2,1)} %bitcast.83, bf16[64,8,4,128]{3,2,1,0:T(4,128)(2,1)} %bitcast.84), kind=kOutput, calls=%fused_computation.34 | convolution fusion | flops 805306368 | bytes 5242880 | tf_op jit(solution)/shard_map/km,kn->mn/dot_general | solution.py:75
  294.3 71.6 %reduce-scatter.2.cloned.1.call-done = f32[64,1536]{1,0:T(8,128)} async-done(((f32[512,1536]{1,0:T(8,128)}), f32[64,1536]{1,0:T(8,128)}) %reduce-scatter.2.cloned.1.call-update) | async-done | bytes 393232 | tf_op jit(solution)/shard_map/reduce_scatter | solution.py:76
  (100 shorter events, 25.8 us)
Async XLA Ops:
  6.5 77.3 %all-gather.2.cloned.1.call-start = ((), (), s32[]{:S(2)}) async-start(), calls=%async_computation.1 | async-start | bytes 4718592 | tf_op jit(solution)/shard_map/all_gather | solution.py:35
  7.3 83.5 %copy-start.4 = (s32[128,4]{0,1:T(4,128)S(1)}, s32[128,4]{0,1:T(4,128)}, u32[]{:S(2)}) copy-start(s32[128,4]{0,1:T(4,128)} %param.9) | copy-start | bytes 6148
  7.3 84.4 %copy-start.5 = (s32[4,27]{1,0:T(4,128)S(1)}, s32[4,27]{1,0:T(4,128)}, u32[]{:S(2)}) copy-start(s32[4,27]{1,0:T(4,128)} %param.7) | copy-start | bytes 1300
  7.3 85.2 %copy-start.1 = (bf16[4,4,128,128]{3,2,1,0:T(8,128)(2,1)S(1)}, bf16[4,4,128,128]{3,2,1,0:T(8,128)(2,1)}, u32[]{:S(2)}) copy-start(bf16[4,4,128,128]{3,2,1,0:T(8,128)(2,1)} %param.8) | copy-start | bytes 1572868
  7.3 358.7 %reduce-scatter.2.cloned.1.call-start = ((), (), s32[]{:S(2)}) async-start(), calls=%async_computation.2 | async-start | bytes 3538944 | tf_op jit(solution)/shard_map/reduce_scatter | solution.py:76
  87.8 48.1 %collective-permute-start = (bf16[16,4,128,128]{3,2,1,0:T(8,128)(2,1)}, bf16[16,4,128,128]{3,2,1,0:T(8,128)(2,1)}, u32[]{:S(2)}, u32[]{:S(2)}) collective-permute-start(bf16[16,4,128,128]{3,2,1,0:T(8,128)(2,1)} %get-tuple-element.71), channel_id=1, source_target_pairs={{0,8},{8,16},{16,24},{24,0},{1,9},{9,17},{17,25},{25,1},{2,10},{10... | collective-permute-start | bytes 6291464 | tf_op jit(solution)/shard_map/ppermute | solution.py:16
  90.8 46.5 %collective-permute-start.1 = (bf16[16,4,128,128]{3,2,1,0:T(8,128)(2,1)S(1)}, bf16[16,4,128,128]{3,2,1,0:T(8,128)(2,1)}, u32[]{:S(2)}, u32[]{:S(2)}) collective-permute-start(bf16[16,4,128,128]{3,2,1,0:T(8,128)(2,1)S(1)} %get-tuple-element.72), channel_id=1, source_target_pairs={{8,0},{16,8},{24,16},{0,24},{9,1},{17,9},{25,17},{1,25},{10,2},{18... | collective-permute-start | bytes 6291464 | tf_op jit(solution)/shard_map/ppermute | solution.py:17
  144.4 4.7 %copy-start.6 = (s32[4,27]{1,0:T(4,128)}, s32[4,27]{1,0:T(4,128)S(1)}, u32[]{:S(2)}) copy-start(s32[4,27]{1,0:T(4,128)S(1)} %get-tuple-element.130) | copy-start | bytes 1300 | tf_op jit(solution)/shard_map/while
  144.4 4.6 %copy-start.2 = (s32[1024]{0:T(1024)}, s32[1024]{0:T(1024)S(1)}, u32[]{:S(2)}) copy-start(s32[1024]{0:T(1024)S(1)} %pad_clamp_fusion.3) | copy-start | bytes 12292 | tf_op jit(solution)/shard_map/while
  149.1 5.8 %copy-start.3 = (pred[27]{0:T(512)(128)(4,1)}, pred[27]{0:T(512)(128)(4,1)S(1)}, u32[]{:S(2)}) copy-start(pred[27]{0:T(512)(128)(4,1)S(1)} %compare_and_fusion.3) | copy-start | bytes 85 | tf_op jit(solution)/shard_map/while
  162.7 7.7 %copy-start = (bf16[27,4,128,128]{2,3,1,0:T(8,128)(2,1)S(1)}, bf16[27,4,128,128]{2,3,1,0:T(8,128)(2,1)}, u32[]{:S(2)}) copy-start(bf16[27,4,128,128]{2,3,1,0:T(8,128)(2,1)} %get-tuple-element.113) | copy-start | bytes 10616836 | tf_op jit(solution)/shard_map/while
  176.3 4.6 %copy-start.7 = (s32[4,27]{1,0:T(4,128)S(1)}, s32[4,27]{1,0:T(4,128)}, u32[]{:S(2)}) copy-start(s32[4,27]{1,0:T(4,128)} %copy-done.6) | copy-start | bytes 1300 | tf_op jit(solution)/shard_map/while
  180.8 4.7 %copy-start.6 = (s32[4,27]{1,0:T(4,128)}, s32[4,27]{1,0:T(4,128)S(1)}, u32[]{:S(2)}) copy-start(s32[4,27]{1,0:T(4,128)S(1)} %get-tuple-element.130) | copy-start | bytes 1300 | tf_op jit(solution)/shard_map/while
  180.9 4.6 %copy-start.2 = (s32[1024]{0:T(1024)}, s32[1024]{0:T(1024)S(1)}, u32[]{:S(2)}) copy-start(s32[1024]{0:T(1024)S(1)} %pad_clamp_fusion.3) | copy-start | bytes 12292 | tf_op jit(solution)/shard_map/while
  185.5 5.8 %copy-start.3 = (pred[27]{0:T(512)(128)(4,1)}, pred[27]{0:T(512)(128)(4,1)S(1)}, u32[]{:S(2)}) copy-start(pred[27]{0:T(512)(128)(4,1)S(1)} %compare_and_fusion.3) | copy-start | bytes 85 | tf_op jit(solution)/shard_map/while
  199.1 7.7 %copy-start = (bf16[27,4,128,128]{2,3,1,0:T(8,128)(2,1)S(1)}, bf16[27,4,128,128]{2,3,1,0:T(8,128)(2,1)}, u32[]{:S(2)}) copy-start(bf16[27,4,128,128]{2,3,1,0:T(8,128)(2,1)} %get-tuple-element.113) | copy-start | bytes 10616836 | tf_op jit(solution)/shard_map/while
  212.7 4.6 %copy-start.7 = (s32[4,27]{1,0:T(4,128)S(1)}, s32[4,27]{1,0:T(4,128)}, u32[]{:S(2)}) copy-start(s32[4,27]{1,0:T(4,128)} %copy-done.6) | copy-start | bytes 1300 | tf_op jit(solution)/shard_map/while
  217.2 4.7 %copy-start.6 = (s32[4,27]{1,0:T(4,128)}, s32[4,27]{1,0:T(4,128)S(1)}, u32[]{:S(2)}) copy-start(s32[4,27]{1,0:T(4,128)S(1)} %get-tuple-element.130) | copy-start | bytes 1300 | tf_op jit(solution)/shard_map/while
  217.3 4.6 %copy-start.2 = (s32[1024]{0:T(1024)}, s32[1024]{0:T(1024)S(1)}, u32[]{:S(2)}) copy-start(s32[1024]{0:T(1024)S(1)} %pad_clamp_fusion.3) | copy-start | bytes 12292 | tf_op jit(solution)/shard_map/while
  221.9 5.8 %copy-start.3 = (pred[27]{0:T(512)(128)(4,1)}, pred[27]{0:T(512)(128)(4,1)S(1)}, u32[]{:S(2)}) copy-start(pred[27]{0:T(512)(128)(4,1)S(1)} %compare_and_fusion.3) | copy-start | bytes 85 | tf_op jit(solution)/shard_map/while
  235.5 7.7 %copy-start = (bf16[27,4,128,128]{2,3,1,0:T(8,128)(2,1)S(1)}, bf16[27,4,128,128]{2,3,1,0:T(8,128)(2,1)}, u32[]{:S(2)}) copy-start(bf16[27,4,128,128]{2,3,1,0:T(8,128)(2,1)} %get-tuple-element.113) | copy-start | bytes 10616836 | tf_op jit(solution)/shard_map/while
  249.1 4.6 %copy-start.7 = (s32[4,27]{1,0:T(4,128)S(1)}, s32[4,27]{1,0:T(4,128)}, u32[]{:S(2)}) copy-start(s32[4,27]{1,0:T(4,128)} %copy-done.6) | copy-start | bytes 1300 | tf_op jit(solution)/shard_map/while
  253.6 4.7 %copy-start.6 = (s32[4,27]{1,0:T(4,128)}, s32[4,27]{1,0:T(4,128)S(1)}, u32[]{:S(2)}) copy-start(s32[4,27]{1,0:T(4,128)S(1)} %get-tuple-element.130) | copy-start | bytes 1300 | tf_op jit(solution)/shard_map/while
  253.7 4.6 %copy-start.2 = (s32[1024]{0:T(1024)}, s32[1024]{0:T(1024)S(1)}, u32[]{:S(2)}) copy-start(s32[1024]{0:T(1024)S(1)} %pad_clamp_fusion.3) | copy-start | bytes 12292 | tf_op jit(solution)/shard_map/while
  258.3 5.8 %copy-start.3 = (pred[27]{0:T(512)(128)(4,1)}, pred[27]{0:T(512)(128)(4,1)S(1)}, u32[]{:S(2)}) copy-start(pred[27]{0:T(512)(128)(4,1)S(1)} %compare_and_fusion.3) | copy-start | bytes 85 | tf_op jit(solution)/shard_map/while
  271.9 7.7 %copy-start = (bf16[27,4,128,128]{2,3,1,0:T(8,128)(2,1)S(1)}, bf16[27,4,128,128]{2,3,1,0:T(8,128)(2,1)}, u32[]{:S(2)}) copy-start(bf16[27,4,128,128]{2,3,1,0:T(8,128)(2,1)} %get-tuple-element.113) | copy-start | bytes 10616836 | tf_op jit(solution)/shard_map/while
  285.5 4.6 %copy-start.7 = (s32[4,27]{1,0:T(4,128)S(1)}, s32[4,27]{1,0:T(4,128)}, u32[]{:S(2)}) copy-start(s32[4,27]{1,0:T(4,128)} %copy-done.6) | copy-start | bytes 1300 | tf_op jit(solution)/shard_map/while
Sparse Core Ops, SparseCore 0:
  9.5 74.2 all-gather.1
  294.4 71.4 reduce-scatter.1
where the time goes:
time: 376 us; the launch traced here: 373 us
  waiting for transfers between devices  192 us (51%)
  local copies, waits for them, and re-layouts  93.6 us (25%)
  matrix products  56.9 us (15%)
  between operations  13.5 us (4%)
  other arithmetic  13.2 us (4%)
    all_gather x1, waiting for transfers between devices, local(): slab_tiles = lax.all_gather(p_tiles, 'col', axis=0, tiled=True)  76.5 us
    reduce_scatter x1, waiting for transfers between devices, local(): lax.psum_scatter(partial_value, 'col', scatter_dimension=0, tiled=True)  71.6 us
    ppermute x1, waiting for transfers between devices, extended_2(): before = lax.ppermute(last, axis, up)  42.2 us
    convert_element_type x4, local copies, waits for them, and re-layouts, row_product(): (products - upper_half.astype(jnp.float32)).astype(jnp.bfloat16)  31.3 us
    convert_element_type x4, local copies, waits for them, and re-layouts, row_product(): upper_half = products.astype(jnp.bfloat16)  23.5 us
    dot_general x4, matrix products, row_product(): jnp.einsum('jab,jqbc->jqac', a_row_tiles, picked, preferred_element_type=...  23 us
    gather x4, local copies, waits for them, and re-layouts, row_product(): picked = jnp.take(extended, row_pos, axis=0)  18.4 us
    dot_general x4, matrix products, row_product(): jnp.einsum('jqw,jqac->awc', window_marks, lower_half, preferred_element_t...  15.5 us
  transfers between devices with their start and end apart: 4, of which 4 were waited for; matrix products, arithmetic and copies ran while one was open for 1% of the time, Pallas kernels for 0%

commit v1 on v0

v1 whole, which is shorter than its diff:
```python
import functools

import jax
import jax.numpy as jnp
from jax import lax
from jax.experimental import pallas as pl
from jax.experimental.pallas import tpu as pltpu
from jax.sharding import PartitionSpec as P

AGG = 8
MESH = pl.DeviceIdType.MESH


def kernel(dims, slots, a_hbm, p_hbm, out, a_scr, p_scr, ad, pt, rowbuf, halo, acc, partf, part16, yrecv, zsend, own,
           zrecv, loc_sem, ag_send, ag_recv, h_send, h_recv, y_send, y_recv, z_send, z_recv):
    R, C, Z, Y, D, KA, KP, B, CBR = dims
    NB = CBR * B
    reach = C // 2
    half = C - reach
    r, c = lax.axis_index("row"), lax.axis_index("col")
    z, y = c // Y, c % Y
    low = c < half
    r_up, r_down = lax.rem(r + 1, R), lax.rem(r + R - 1, R)

    def dev(row, col):
        return {"row": row, "col": col}

    copy_p = pltpu.make_async_copy(p_hbm, p_scr.at[:, pl.ds(0, KP)], loc_sem.at[0])
    copy_a = pltpu.make_async_copy(a_hbm, a_scr.at[:, pl.ds(0, KA)], loc_sem.at[1])
    copy_p.start()
    copy_a.start()
    barrier = pltpu.get_barrier_semaphore()
    for k in range(1, Z):
        pl.semaphore_signal(barrier, inc=1, device_id=dev(r, lax.rem(z + k, Z) * Y + y), device_id_type=MESH)
    if Y == 2:
        pl.semaphore_signal(barrier, inc=1, device_id=dev(r, z * Y + 1 - y), device_id_type=MESH)
    pl.semaphore_signal(barrier, inc=1, device_id=dev(r_up, c), device_id_type=MESH)
    pl.semaphore_signal(barrier, inc=1, device_id=dev(r_down, c), device_id_type=MESH)

    for i in range(D):
        p_scr[i, KP] = jnp.zeros((B, B), jnp.bfloat16)
        a_scr[i, KA] = jnp.zeros((B, B), jnp.bfloat16)
    copy_p.wait()
    for i in range(D):
        for m in range(CBR):
            rowbuf[c, i * B:(i + 1) * B, m * B:(m + 1) * B] = p_scr[i, slots[i, m]]
    pl.semaphore_wait(barrier, Z - 1 + (Y - 1) + 2)

    def ag_copy(kind, slab, col):
        return pltpu.make_async_remote_copy(
            src_ref=rowbuf.at[slab], dst_ref=rowbuf.at[slab], send_sem=ag_send.at[kind, slab],
            recv_sem=ag_recv.at[slab], device_id=dev(r, col), device_id_type=MESH)

    def halo_copy(slab, idx, row):
        return pltpu.make_async_remote_copy(
            src_ref=rowbuf.at[slab], dst_ref=halo.at[idx], send_sem=h_send.at[idx],
            recv_sem=h_recv.at[idx], device_id=dev(row, c), device_id_type=MESH)

    def halo_forward(slab):
        @pl.when(jnp.logical_and(low, slab >= c + half))
        def _():
            halo_copy(slab, slab - half, r_up).start()

        @pl.when(jnp.logical_and(jnp.logical_not(low), slab <= c - reach))
        def _():
            halo_copy(slab, slab, r_down).start()

    def use(buf, slab, d, band):
        for n in range(0, NB, 256):
            acc[band, :, n:n + 256] += jnp.dot(ad[d + reach], buf[slab, :, n:n + 256],
                                               preferred_element_type=jnp.float32)

    def use_row(slab):
        d = slab - c

        @pl.when(jnp.logical_and(d <= reach, d >= -reach))
        def _():
            use(rowbuf, slab, d, 0)

    @pl.when(z + 1 < Z)
    def _():
        ag_copy(0, c, c + Y).start()

    @pl.when(z > 0)
    def _():
        ag_copy(1, c, c - Y).start()

    if Y == 2:
        ag_copy(2, c, z * Y + 1 - y).start()

    acc[...] = jnp.zeros_like(acc)
    copy_a.wait()

    def build(d, carry):
        for i in range(D):
            for s in range(D):
                ad[d, i * B:(i + 1) * B, s * B:(s + 1) * B] = a_scr[i, slots[i, CBR + d * D + s]]
        return carry

    lax.fori_loop(0, 2 * reach + 1, build, 0)
    pt[...] = rowbuf[c].T
    use(rowbuf, c, 0, 0)

    def line(k, carry):
        below, above = z - k, z + k
        for there, ok in ((below, below >= 0), (above, above < Z)):
            slab = there * Y + y

            @pl.when(ok)
            def _():
                ag_copy(0, slab, c).wait_recv()
                if there is below:
                    @pl.when(z + 1 < Z)
                    def _():
                        ag_copy(0, slab, c + Y).start()
                else:
                    @pl.when(z > 0)
                    def _():
                        ag_copy(1, slab, c - Y).start()
                if Y == 2:
                    ag_copy(2, slab, z * Y + 1 - y).start()
                halo_forward(slab)
        for there, ok in ((below, below >= 0), (above, above < Z)):
            @pl.when(ok)
            def _():
                use_row(there * Y + y)
        if Y == 2:
            for there, ok in ((z - k + 1, z - k + 1 >= 0), (z + k - 1, jnp.logical_and(z + k - 1 < Z, k > 1))):
                @pl.when(ok)
                def _():
                    slab = there * Y + 1 - y
                    ag_copy(2, slab, c).wait_recv()
                    halo_forward(slab)
                    use_row(slab)
        return carry

    lax.fori_loop(1, Z + Y - 1, line, 0)

    def y_copy(band):
        return pltpu.make_async_remote_copy(
            src_ref=part16.at[band], dst_ref=yrecv.at[band], send_sem=y_send.at[band],
            recv_sem=y_recv.at[band], device_id=dev(r, z * Y + 1 - y), device_id_type=MESH)

    share = NB // C

    def partial(band):
        for n in range(0, NB, 256):
            ap = acc[band, :, n:n + 256].astype(jnp.bfloat16)
            res = jnp.dot(pt[...], ap, preferred_element_type=jnp.float32)
            for t in range(C):
                partf[band, t % Y, t // Y, :, n:n + 256] = res[t * share:(t + 1) * share]
        if Y == 2:
            part16[band] = partf[band, 1 - y].astype(jnp.bfloat16)
            y_copy(band).start()

    partial(0)

    def halo_use(t, carry):
        idx = jnp.where(low, t, reach - 1 - t)

        @pl.when(jnp.logical_or(jnp.logical_and(low, idx >= c), jnp.logical_and(jnp.logical_not(low), idx <= c - reach)))
        def _():
            halo_copy(c, idx, r_up).wait_recv()
            use(halo, idx, jnp.where(low, idx - reach - c, C + idx - c), 1)
        return carry

    lax.fori_loop(0, reach, halo_use, 0)
    partial(1)

    def z_copy(band, to, slot):
        return pltpu.make_async_remote_copy(
            src_ref=zsend.at[band, to], dst_ref=zrecv.at[band, slot], send_sem=z_send.at[band, to],
            recv_sem=z_recv.at[band, slot], device_id=dev(r, to * Y + y), device_id_type=MESH)

    for band in range(2):
        if Y == 2:
            y_copy(band).wait_recv()
            own[band] = partf[band, y, z] + yrecv[band, z].astype(jnp.float32)
        else:
            own[band] = partf[band, y, z]
        for t in range(Z):
            @pl.when(t != z)
            def _():
                total = partf[band, y, t]
                if Y == 2:
                    total = total + yrecv[band, t].astype(jnp.float32)
                zsend[band, t] = total.astype(jnp.bfloat16)
                z_copy(band, t, z).start()

    out[...] = jnp.zeros_like(out)
    out[:, NB:2 * NB] = own[0]

    @pl.when(low)
    def _():
        out[:, 0:NB] = own[1]

    @pl.when(jnp.logical_not(low))
    def _():
        out[:, 2 * NB:3 * NB] = own[1]

    for band in range(2):
        for t in range(Z):
            start = NB if band == 0 else (0 if t < Z // 2 else 2 * NB)

            @pl.when(t != z)
            def _():
                z_copy(band, t, t).wait_recv()
                out[:, start:start + NB] += zrecv[band, t].astype(jnp.float32)

    for band in range(2):
        if Y == 2:
            y_copy(band).wait_send()
        for t in range(Z):
            @pl.when(t != z)
            def _():
                z_copy(band, t, z).wait_send()

    def drain(slab, carry):
        mine = slab % Y == y
        there = slab // Y

        @pl.when(jnp.logical_and(mine, jnp.logical_and(there <= z, z + 1 < Z)))
        def _():
            ag_copy(0, slab, c).wait_send()

        @pl.when(jnp.logical_and(mine, jnp.logical_and(there >= z, z > 0)))
        def _():
            ag_copy(1, slab, c).wait_send()

        if Y == 2:
            @pl.when(mine)
            def _():
                ag_copy(2, slab, c).wait_send()

        @pl.when(jnp.logical_and(low, slab >= c + half))
        def _():
            halo_copy(slab, slab - half, r_up).wait_send()

        @pl.when(jnp.logical_and(jnp.logical_not(low), slab <= c - reach))
        def _():
            halo_copy(slab, slab, r_down).wait_send()
        return carry

    lax.fori_loop(0, C, drain, 0)


def local(Y, a_tiles, a_cols, p_tiles, p_cols):
    D, KA, B = a_tiles.shape[:3]
    KP = p_tiles.shape[1]
    C, R = lax.axis_size("col"), lax.axis_size("row")
    Z = C // Y
    slab_len = D * C
    total_rows = slab_len * R
    CBR = slab_len // AGG
    NB = CBR * B
    reach = slab_len // 2
    rs = C // 2
    first_row = (lax.axis_index("row") * C + lax.axis_index("col")) * D
    own_cols = lax.dynamic_slice_in_dim(p_cols, first_row, D, 0) % CBR
    m_ids = jnp.arange(CBR, dtype=jnp.int32)
    q_ids = KP - jnp.arange(KP, dtype=jnp.int32)
    p_slot = KP - jnp.sum(jnp.where(own_cols[:, :, None] == m_ids, q_ids[:, None], 0), axis=1)
    rel = (a_cols - first_row + reach) % total_rows
    e_ids = jnp.arange(2 * reach + D, dtype=jnp.int32)
    j_ids = KA - jnp.arange(KA, dtype=jnp.int32)
    a_slot = KA - jnp.sum(jnp.where(rel[:, :, None] == e_ids, j_ids[:, None], 0), axis=1)
    slots = jnp.concatenate([p_slot, a_slot], axis=1)
    bf, f32 = jnp.bfloat16, jnp.float32
    share = NB // C
    S = pltpu.SemaphoreType.DMA
    V = pltpu.VMEM
    return pl.pallas_call(
        functools.partial(kernel, (R, C, Z, Y, D, KA, KP, B, CBR)),
        out_shape=jax.ShapeDtypeStruct((share, 3 * NB), f32),
        in_specs=[pl.BlockSpec(memory_space=pltpu.SMEM), pl.BlockSpec(memory_space=pl.ANY),
                  pl.BlockSpec(memory_space=pl.ANY)],
        out_specs=pl.BlockSpec(memory_space=pltpu.VMEM),
        scratch_shapes=[
            V((D, KA + 1, B, B), bf), V((D, KP + 1, B, B), bf),
            V((2 * rs + 1, D * B, D * B), bf), V((NB, D * B), bf),
            V((C, D * B, NB), bf), V((rs, D * B, NB), bf),
            V((2, D * B, NB), f32), V((2, Y, Z, share, NB), f32),
            V((2, Z, share, NB), bf), V((2, Z, share, NB), bf),
            V((2, Z, share, NB), bf), V((2, share, NB), f32), V((2, Z, share, NB), bf),
            S((2,)), S((3, C)), S((C,)), S((rs,)), S((rs,)), S((2,)), S((2,)), S((2, Z)), S((2, Z)),
        ],
        compiler_params=pltpu.CompilerParams(collective_id=0, has_side_effects=True,
                                             vmem_limit_bytes=60 * 1024 * 1024),
    )(slots, a_tiles, p_tiles)


def solution(mesh):
    Y = 2 if mesh.shape["groups"] == 1 else 1
    in_specs = (
        P(("groups", "row", "col"), None, None, None),
        P(("groups", "row", "col"), None),
        P(("groups", "row", "col"), None, None, None),
        P("groups", None),
    )
    out_specs = P(("groups", "row", "col"), None)
    return jax.shard_map(functools.partial(local, Y), mesh=mesh, in_specs=in_specs, out_specs=out_specs,
                         check_vma=False)
```

time: 376 us -> 77.4 us (0.21)
  waiting for transfers between devices: 192 us -> 0 us
  local copies, waits for them, and re-layouts: 93.6 us -> 2.04 us
  Pallas kernels: 0 us -> 72.5 us
  matrix products: 56.9 us -> 0 us
  between operations: 13.5 us -> 0.03 us
  other arithmetic: 13.2 us -> 1.6 us
    all_gather x1 -> x0, waiting for transfers between devices: 76.5 us -> none  [local(): slab_tiles = lax.all_gather(p_tiles, 'col', axis=0, tiled=True)]
    pallas_call x0 -> x1, Pallas kernels: none -> 72.5 us  [local(): pl.pallas_call(functools.partial(kernel, (R, C, Z, Y, D, KA, KP, B, CBR))...]
    reduce_scatter x1 -> x0, waiting for transfers between devices: 71.6 us -> none  [local(): lax.psum_scatter(partial_value, 'col', scatter_dimension=0, tiled=True)]
    dot_general x14 -> x0, matrix products: 56.9 us -> none  [the longest x4 23 us: row_product(): jnp.einsum('jab,jqbc->jqac', a_row_tiles, picked, preferred_element_type=...]
    convert_element_type x12 -> x0, local copies, waits for them, and re-layouts: 56.4 us -> none  [the longest x4 31.3 us: row_product(): (products - upper_half.astype(jnp.float32)).astype(jnp.bfloat16)]
    ppermute x2 -> x0, waiting for transfers between devices: 43.5 us -> none  [the longest x1 42.2 us: extended_2(): before = lax.ppermute(last, axis, up)]
    gather x9 -> x0, local copies, waits for them, and re-layouts: 25.9 us -> none  [the longest x4 18.4 us: row_product(): picked = jnp.take(extended, row_pos, axis=0)]
    concatenate x1, other arithmetic: 7.18 us -> 0.65 us  [local(): slots = jnp.concatenate([p_slot, a_slot], axis=1)]
  transfers between devices with their start and end apart: 4 -> 0, of which waited for: 4 -> 0; matrix products, arithmetic and copies ran while one was open for 1% -> 0% of each run, Pallas kernels for 0% -> 0%
where the time goes in v1:
time: 77.4 us; the launch traced here: 76.1 us
  Pallas kernels  72.5 us (94%)
  local copies, waits for them, and re-layouts  2.04 us (3%)
  other arithmetic  1.6 us (2%)
    pallas_call x1, Pallas kernels, local(): pl.pallas_call(functools.partial(kernel, (R, C, Z, Y, D, KA, KP, B, CBR))...  72.5 us
    unnamed x4, local copies, waits for them, and re-layouts  1.87 us

profile of v1, /device:TPU:1, one launch (start us, length us, event | category | flops | bytes accessed | tf_op | source)
XLA Modules:
  0.0 76.1 jit_solution(9876368947157097454)
XLA Ops:
  0.0 0.0 copy-start
  0.0 0.7 add_select_fusion
  0.7 0.0 copy-done
  0.7 0.1 constant_dynamic-slice_fusion
  0.8 0.1 copy.8
  0.9 0.1 select_reduce_fusion.1
  1.0 0.1 copy.7
  1.1 0.1 select_reduce_fusion
  1.2 0.7 pad_add_fusion.slots
  1.9 72.5 %shard_map.46 = f32[64,1536]{1,0:T(8,128)} custom-call(s32[4,40]{1,0:T(4,128)} %pad_add_fusion.slots, bf16[4,27,128,128]{3,2,1,0:T(8,128)(2,1)} %a_hbm.1, bf16[4,4,128,128]{3,2,1,0:T(8,128)(2,1)} %p_hbm.1), custom_call_target="tpu_custom_call" | custom-call | tf_op jit(solution)/shard_map/pallas_call | solution.py:272
  74.4 1.8 %copy.10 = f32[64,1536]{1,0:T(8,128)} copy(f32[64,1536]{1,0:T(8,128)} %shard_map.46) | data formatting | bytes 786432
  (5 shorter events, 0.0 us)
Async XLA Ops:
  0.0 0.7 copy-start

commit v2 on v1

--- a/solution.py
+++ b/solution.py
@@ -46,24 +46,76 @@
             rowbuf[c, i * B:(i + 1) * B, m * B:(m + 1) * B] = p_scr[i, slots[i, m]]
     pl.semaphore_wait(barrier, Z - 1 + (Y - 1) + 2)
 
-    def ag_copy(kind, slab, col):
+    H = 2
+    hb = D * B // H
+
+    def piece(h):
+        return pl.ds(pl.multiple_of(h * hb, hb), hb)
+
+    def ag_copy(kind, slab, h, col):
         return pltpu.make_async_remote_copy(
-            src_ref=rowbuf.at[slab], dst_ref=rowbuf.at[slab], send_sem=ag_send.at[kind, slab],
-            recv_sem=ag_recv.at[slab], device_id=dev(r, col), device_id_type=MESH)
-
-    def halo_copy(slab, idx, row):
+            src_ref=rowbuf.at[slab, piece(h)], dst_ref=rowbuf.at[slab, piece(h)], send_sem=ag_send.at[kind, slab, h],
+            recv_sem=ag_recv.at[slab, h], device_id=dev(r, col), device_id_type=MESH)
+
+    def halo_copy(slab, idx, h, row):
         return pltpu.make_async_remote_copy(
-            src_ref=rowbuf.at[slab], dst_ref=halo.at[idx], send_sem=h_send.at[idx],
-            recv_sem=h_recv.at[idx], device_id=dev(row, c), device_id_type=MESH)
-
-    def halo_forward(slab):
-        @pl.when(jnp.logical_and(low, slab >= c + half))
-        def _():
-            halo_copy(slab, slab - half, r_up).start()
-
-        @pl.when(jnp.logical_and(jnp.logical_not(low), slab <= c - reach))
-        def _():
-            halo_copy(slab, slab, r_down).start()
+            src_ref=rowbuf.at[slab, piece(h)], dst_ref=halo.at[idx, piece(h)], send_sem=h_send.at[idx, h],
+            recv_sem=h_recv.at[idx, h], device_id=dev(row, c), device_id_type=MESH)
+
+    def when(*conds):
+        return pl.when(functools.reduce(jnp.logical_and, conds))
+
+    def up_ok(slab, h):
+        mine, there = slab % Y == y, slab // Y
+        by_line = jnp.logical_or(mine, there == 0) if h == H - 1 else mine
+        return functools.reduce(jnp.logical_and, (by_line, there <= z, z + 1 < Z))
+
+    def down_ok(slab, h):
+        mine, there = slab % Y == y, slab // Y
+        by_line = jnp.logical_or(mine, there == Z - 1) if h == H - 1 else mine
+        return functools.reduce(jnp.logical_and, (by_line, there >= z, z > 0))
+
+    def y_ok(slab, h):
+        mine, there = slab % Y == y, slab // Y
+        if h == H - 1:
+            inner = jnp.logical_and(there > 0, there < Z - 1)
+            return jnp.logical_and(mine, jnp.logical_or(slab == c, inner))
+        return mine
+
+    def halo_up(slab):
+        return jnp.logical_and(low, slab >= c + half)
+
+    def halo_down(slab):
+        return jnp.logical_and(jnp.logical_not(low), slab <= c - reach)
+
+    def each(slab, h, act):
+        @pl.when(up_ok(slab, h))
+        def _():
+            act(ag_copy(0, slab, h, c + Y))
+
+        @pl.when(down_ok(slab, h))
+        def _():
+            act(ag_copy(1, slab, h, c - Y))
+
+        if Y == 2:
+            @pl.when(y_ok(slab, h))
+            def _():
+                act(ag_copy(2, slab, h, z * Y + 1 - y))
+
+        @pl.when(halo_up(slab))
+        def _():
+            act(halo_copy(slab, slab - half, h, r_up))
+
+        @pl.when(halo_down(slab))
+        def _():
+            act(halo_copy(slab, slab, h, r_down))
+
+    def start(copy):
+        copy.start()
+
+    def receive(slab, h):
+        ag_copy(0, slab, h, c).wait_recv()
+        each(slab, h, start)
 
     def use(buf, slab, d, band):
         for n in range(0, NB, 256):
@@ -77,16 +129,8 @@
         def _():
             use(rowbuf, slab, d, 0)
 
-    @pl.when(z + 1 < Z)
-    def _():
-        ag_copy(0, c, c + Y).start()
-
-    @pl.when(z > 0)
-    def _():
-        ag_copy(1, c, c - Y).start()
-
-    if Y == 2:
-        ag_copy(2, c, z * Y + 1 - y).start()
+    for h in range(H):
+        each(c, h, start)
 
     acc[...] = jnp.zeros_like(acc)
     copy_a.wait()
@@ -100,41 +144,6 @@
     lax.fori_loop(0, 2 * reach + 1, build, 0)
     pt[...] = rowbuf[c].T
     use(rowbuf, c, 0, 0)
-
-    def line(k, carry):
-        below, above = z - k, z + k
-        for there, ok in ((below, below >= 0), (above, above < Z)):
-            slab = there * Y + y
-
-            @pl.when(ok)
-            def _():
-                ag_copy(0, slab, c).wait_recv()
-                if there is below:
-                    @pl.when(z + 1 < Z)
-                    def _():
-                        ag_copy(0, slab, c + Y).start()
-                else:
-                    @pl.when(z > 0)
-                    def _():
-                        ag_copy(1, slab, c - Y).start()
-                if Y == 2:
-                    ag_copy(2, slab, z * Y + 1 - y).start()
-                halo_forward(slab)
-        for there, ok in ((below, below >= 0), (above, above < Z)):
-            @pl.when(ok)
-            def _():
-                use_row(there * Y + y)
-        if Y == 2:
-            for there, ok in ((z - k + 1, z - k + 1 >= 0), (z + k - 1, jnp.logical_and(z + k - 1 < Z, k > 1))):
-                @pl.when(ok)
-                def _():
-                    slab = there * Y + 1 - y
-                    ag_copy(2, slab, c).wait_recv()
-                    halo_forward(slab)
-                    use_row(slab)
-        return carry
-
-    lax.fori_loop(1, Z + Y - 1, line, 0)
 
     def y_copy(band):
         return pltpu.make_async_remote_copy(
@@ -153,14 +162,43 @@
             part16[band] = partf[band, 1 - y].astype(jnp.bfloat16)
             y_copy(band).start()
 
-    partial(0)
+    def line(k, carry):
+        pairs = ((z - k, z - k >= 0), (z + k, z + k < Z))
+        cross = ((z - k + 1, z - k + 1 >= 0), (z + k - 1, jnp.logical_and(z + k - 1 < Z, k > 1)))
+        for h in range(H):
+            for there, ok in pairs:
+                @pl.when(ok)
+                def _():
+                    receive(there * Y + y, h)
+            if Y == 2:
+                for there, ok in cross:
+                    @pl.when(ok)
+                    def _():
+                        receive(there * Y + 1 - y, h)
+        for there, ok in pairs:
+            @pl.when(ok)
+            def _():
+                use_row(there * Y + y)
+        if Y == 2:
+            for there, ok in cross:
+                @pl.when(ok)
+                def _():
+                    use_row(there * Y + 1 - y)
+
+        @pl.when(k == Z // 2 + Y - 1)
+        def _():
+            partial(0)
+        return carry
+
+    lax.fori_loop(1, Z + Y - 1, line, 0)
 
     def halo_use(t, carry):
         idx = jnp.where(low, t, reach - 1 - t)
 
         @pl.when(jnp.logical_or(jnp.logical_and(low, idx >= c), jnp.logical_and(jnp.logical_not(low), idx <= c - reach)))
         def _():
-            halo_copy(c, idx, r_up).wait_recv()
+            for h in range(H):
+                halo_copy(c, idx, h, r_up).wait_recv()
             use(halo, idx, jnp.where(low, idx - reach - c, C + idx - c), 1)
         return carry
 
@@ -216,29 +254,8 @@
                 z_copy(band, t, z).wait_send()
 
     def drain(slab, carry):
-        mine = slab % Y == y
-        there = slab // Y
-
-        @pl.when(jnp.logical_and(mine, jnp.logical_and(there <= z, z + 1 < Z)))
-        def _():
-            ag_copy(0, slab, c).wait_send()
-
-        @pl.when(jnp.logical_and(mine, jnp.logical_and(there >= z, z > 0)))
-        def _():
-            ag_copy(1, slab, c).wait_send()
-
-        if Y == 2:
-            @pl.when(mine)
-            def _():
-                ag_copy(2, slab, c).wait_send()
-
-        @pl.when(jnp.logical_and(low, slab >= c + half))
-        def _():
-            halo_copy(slab, slab - half, r_up).wait_send()
-
-        @pl.when(jnp.logical_and(jnp.logical_not(low), slab <= c - reach))
-        def _():
-            halo_copy(slab, slab, r_down).wait_send()
+        for h in range(H):
+            each(slab, h, lambda copy: copy.wait_send())
         return carry
 
     lax.fori_loop(0, C, drain, 0)
@@ -259,11 +276,11 @@
     own_cols = lax.dynamic_slice_in_dim(p_cols, first_row, D, 0) % CBR
     m_ids = jnp.arange(CBR, dtype=jnp.int32)
     q_ids = KP - jnp.arange(KP, dtype=jnp.int32)
-    p_slot = KP - jnp.sum(jnp.where(own_cols[:, :, None] == m_ids, q_ids[:, None], 0), axis=1)
+    p_slot = KP - jnp.max(jnp.where(own_cols[:, :, None] == m_ids, q_ids[:, None], 0), axis=1)
     rel = (a_cols - first_row + reach) % total_rows
     e_ids = jnp.arange(2 * reach + D, dtype=jnp.int32)
     j_ids = KA - jnp.arange(KA, dtype=jnp.int32)
-    a_slot = KA - jnp.sum(jnp.where(rel[:, :, None] == e_ids, j_ids[:, None], 0), axis=1)
+    a_slot = KA - jnp.max(jnp.where(rel[:, :, None] == e_ids, j_ids[:, None], 0), axis=1)
     slots = jnp.concatenate([p_slot, a_slot], axis=1)
     bf, f32 = jnp.bfloat16, jnp.float32
     share = NB // C
@@ -282,7 +299,7 @@
             V((2, D * B, NB), f32), V((2, Y, Z, share, NB), f32),
             V((2, Z, share, NB), bf), V((2, Z, share, NB), bf),
             V((2, Z, share, NB), bf), V((2, share, NB), f32), V((2, Z, share, NB), bf),
-            S((2,)), S((3, C)), S((C,)), S((rs,)), S((rs,)), S((2,)), S((2,)), S((2, Z)), S((2, Z)),
+            S((2,)), S((3, C, 2)), S((C, 2)), S((rs, 2)), S((rs, 2)), S((2,)), S((2,)), S((2, Z)), S((2, Z)),
         ],
         compiler_params=pltpu.CompilerParams(collective_id=0, has_side_effects=True,
                                              vmem_limit_bytes=60 * 1024 * 1024),

time: 77.4 us -> 70.2 us (0.907); the launches traced: 76.1 us -> 70 us
  Pallas kernels: 72.5 us -> 66.3 us
    pallas_call x1, Pallas kernels: 72.5 us -> 66.3 us  [local(): pl.pallas_call(functools.partial(kernel, (R, C, Z, Y, D, KA, KP, B, CBR))...]
where the time goes in v2:
time: 70.2 us; the launch traced here: 70 us
  Pallas kernels  66.3 us (94%)
  local copies, waits for them, and re-layouts  2.04 us (3%)
  other arithmetic  1.6 us (2%)
    pallas_call x1, Pallas kernels, local(): pl.pallas_call(functools.partial(kernel, (R, C, Z, Y, D, KA, KP, B, CBR))...  66.3 us
    unnamed x4, local copies, waits for them, and re-layouts  1.87 us

profile of v2, /device:TPU:1, one launch (start us, length us, event | category | flops | bytes accessed | tf_op | source)
XLA Modules:
  0.0 70.0 jit_solution(6625652707770422018)
XLA Ops:
  0.0 0.0 copy-start
  0.0 0.7 add_select_fusion
  0.7 0.0 copy-done
  0.7 0.1 constant_dynamic-slice_fusion
  0.8 0.1 copy.8
  0.9 0.1 select_reduce_fusion.1
  1.0 0.1 copy.7
  1.1 0.1 select_reduce_fusion
  1.2 0.7 pad_add_fusion.slots
  1.9 66.3 %shard_map.46 = f32[64,1536]{1,0:T(8,128)} custom-call(s32[4,40]{1,0:T(4,128)} %pad_add_fusion.slots, bf16[4,27,128,128]{3,2,1,0:T(8,128)(2,1)} %a_hbm.1, bf16[4,4,128,128]{3,2,1,0:T(8,128)(2,1)} %p_hbm.1), custom_call_target="tpu_custom_call" | custom-call | tf_op jit(solution)/shard_map/pallas_call | solution.py:289
  68.2 1.8 %copy.10 = f32[64,1536]{1,0:T(8,128)} copy(f32[64,1536]{1,0:T(8,128)} %shard_map.46) | data formatting | bytes 786432
  (5 shorter events, 0.0 us)
Async XLA Ops:
  0.0 0.7 %copy-start = (s32[128,4]{0,1:T(4,128)S(1)}, s32[128,4]{0,1:T(4,128)}, u32[]{:S(2)}) copy-start(s32[128,4]{0,1:T(4,128)} %param.7) | copy-start | bytes 6148

commit v3 on v2

--- a/solution.py
+++ b/solution.py
@@ -46,7 +46,7 @@
             rowbuf[c, i * B:(i + 1) * B, m * B:(m + 1) * B] = p_scr[i, slots[i, m]]
     pl.semaphore_wait(barrier, Z - 1 + (Y - 1) + 2)
 
-    H = 2
+    H = 4
     hb = D * B // H
 
     def piece(h):
@@ -67,17 +67,17 @@
 
     def up_ok(slab, h):
         mine, there = slab % Y == y, slab // Y
-        by_line = jnp.logical_or(mine, there == 0) if h == H - 1 else mine
+        by_line = jnp.logical_or(mine, there == 0) if h >= H // 2 else mine
         return functools.reduce(jnp.logical_and, (by_line, there <= z, z + 1 < Z))
 
     def down_ok(slab, h):
         mine, there = slab % Y == y, slab // Y
-        by_line = jnp.logical_or(mine, there == Z - 1) if h == H - 1 else mine
+        by_line = jnp.logical_or(mine, there == Z - 1) if h >= H // 2 else mine
         return functools.reduce(jnp.logical_and, (by_line, there >= z, z > 0))
 
     def y_ok(slab, h):
         mine, there = slab % Y == y, slab // Y
-        if h == H - 1:
+        if h >= H // 2:
             inner = jnp.logical_and(there > 0, there < Z - 1)
             return jnp.logical_and(mine, jnp.logical_or(slab == c, inner))
         return mine
@@ -129,10 +129,12 @@
         def _():
             use(rowbuf, slab, d, 0)
 
-    for h in range(H):
+    for h in (2, 3, 0, 1):
         each(c, h, start)
 
     acc[...] = jnp.zeros_like(acc)
+    for n in range(NB // 256):
+        zrecv[1, n, z] = jnp.zeros(zrecv.shape[3:], jnp.bfloat16)
     copy_a.wait()
 
     def build(d, carry):
@@ -145,27 +147,50 @@
     pt[...] = rowbuf[c].T
     use(rowbuf, c, 0, 0)
 
-    def y_copy(band):
+    share = NB // C
+    width = 256
+    parts = NB // width
+
+    def y_copy(band, n):
         return pltpu.make_async_remote_copy(
-            src_ref=part16.at[band], dst_ref=yrecv.at[band], send_sem=y_send.at[band],
-            recv_sem=y_recv.at[band], device_id=dev(r, z * Y + 1 - y), device_id_type=MESH)
-
-    share = NB // C
+            src_ref=part16.at[band, n], dst_ref=yrecv.at[band, n], send_sem=y_send.at[band, n],
+            recv_sem=y_recv.at[band, n], device_id=dev(r, z * Y + 1 - y), device_id_type=MESH)
+
+    def z_copy(band, n, to, slot):
+        return pltpu.make_async_remote_copy(
+            src_ref=zsend.at[band, n, to], dst_ref=zrecv.at[band, n, slot], send_sem=z_send.at[band, n, to],
+            recv_sem=z_recv.at[band, n, slot], device_id=dev(r, to * Y + y), device_id_type=MESH)
 
     def partial(band):
-        for n in range(0, NB, 256):
-            ap = acc[band, :, n:n + 256].astype(jnp.bfloat16)
+        for n in range(parts):
+            ap = acc[band, :, n * width:(n + 1) * width].astype(jnp.bfloat16)
             res = jnp.dot(pt[...], ap, preferred_element_type=jnp.float32)
             for t in range(C):
-                partf[band, t % Y, t // Y, :, n:n + 256] = res[t * share:(t + 1) * share]
-        if Y == 2:
-            part16[band] = partf[band, 1 - y].astype(jnp.bfloat16)
-            y_copy(band).start()
+                partf[band, n, t % Y, t // Y] = res[t * share:(t + 1) * share]
+            if Y == 2:
+                part16[band, n] = partf[band, n, 1 - y].astype(jnp.bfloat16)
+                y_copy(band, n).start()
+
+    def spread(band):
+        for n in range(parts):
+            if Y == 2:
+                y_copy(band, n).wait_recv()
+            for k in range(1, Z):
+                t = lax.rem(z + k, Z)
+                total = partf[band, n, y, t]
+                if Y == 2:
+                    total = total + yrecv[band, n, t].astype(jnp.float32)
+                zsend[band, n, t] = total.astype(jnp.bfloat16)
+                z_copy(band, n, t, z).start()
+            total = partf[band, n, y, z]
+            if Y == 2:
+                total = total + yrecv[band, n, z].astype(jnp.float32)
+            own[band, n] = total
 
     def line(k, carry):
         pairs = ((z - k, z - k >= 0), (z + k, z + k < Z))
         cross = ((z - k + 1, z - k + 1 >= 0), (z + k - 1, jnp.logical_and(z + k - 1 < Z, k > 1)))
-        for h in range(H):
+        for h in (2, 3, 0, 1):
             for there, ok in pairs:
                 @pl.when(ok)
                 def _():
@@ -205,53 +230,41 @@
     lax.fori_loop(0, reach, halo_use, 0)
     partial(1)
 
-    def z_copy(band, to, slot):
-        return pltpu.make_async_remote_copy(
-            src_ref=zsend.at[band, to], dst_ref=zrecv.at[band, slot], send_sem=z_send.at[band, to],
-            recv_sem=z_recv.at[band, slot], device_id=dev(r, to * Y + y), device_id_type=MESH)
+    spread(0)
+    spread(1)
+
+    def place(band, n, first):
+        columns = slice(first + n * width, first + (n + 1) * width)
+        total = own[band, n]
+        for k in range(1, Z):
+            t = lax.rem(z + k, Z)
+            z_copy(band, n, t, t).wait_recv()
+            total += zrecv[band, n, t].astype(jnp.float32)
+        out[:, columns] = total
+
+    def place_sides(n):
+        for k in range(1, Z):
+            t = lax.rem(z + k, Z)
+            z_copy(1, n, t, t).wait_recv()
+        mine = own[1, n]
+        for side in range(2):
+            first = side * 2 * NB + n * width
+            total = jnp.where(low == (side == 0), mine, 0.0)
+            for t in range(side * (Z // 2), (side + 1) * (Z // 2)):
+                total += zrecv[1, n, t].astype(jnp.float32)
+            out[:, first:first + width] = total
+
+    for n in range(parts):
+        place(0, n, NB)
+    for n in range(parts):
+        place_sides(n)
 
     for band in range(2):
-        if Y == 2:
-            y_copy(band).wait_recv()
-            own[band] = partf[band, y, z] + yrecv[band, z].astype(jnp.float32)
-        else:
-            own[band] = partf[band, y, z]
-        for t in range(Z):
-            @pl.when(t != z)
-            def _():
-                total = partf[band, y, t]
-                if Y == 2:
-                    total = total + yrecv[band, t].astype(jnp.float32)
-                zsend[band, t] = total.astype(jnp.bfloat16)
-                z_copy(band, t, z).start()
-
-    out[...] = jnp.zeros_like(out)
-    out[:, NB:2 * NB] = own[0]
-
-    @pl.when(low)
-    def _():
-        out[:, 0:NB] = own[1]
-
-    @pl.when(jnp.logical_not(low))
-    def _():
-        out[:, 2 * NB:3 * NB] = own[1]
-
-    for band in range(2):
-        for t in range(Z):
-            start = NB if band == 0 else (0 if t < Z // 2 else 2 * NB)
-
-            @pl.when(t != z)
-            def _():
-                z_copy(band, t, t).wait_recv()
-                out[:, start:start + NB] += zrecv[band, t].astype(jnp.float32)
-
-    for band in range(2):
-        if Y == 2:
-            y_copy(band).wait_send()
-        for t in range(Z):
-            @pl.when(t != z)
-            def _():
-                z_copy(band, t, z).wait_send()
+        for n in range(parts):
+            if Y == 2:
+                y_copy(band, n).wait_send()
+            for k in range(1, Z):
+                z_copy(band, n, lax.rem(z + k, Z), z).wait_send()
 
     def drain(slab, carry):
         for h in range(H):
@@ -284,6 +297,8 @@
     slots = jnp.concatenate([p_slot, a_slot], axis=1)
     bf, f32 = jnp.bfloat16, jnp.float32
     share = NB // C
+    width = 256
+    N = NB // width
     S = pltpu.SemaphoreType.DMA
     V = pltpu.VMEM
     return pl.pallas_call(
@@ -296,10 +311,10 @@
             V((D, KA + 1, B, B), bf), V((D, KP + 1, B, B), bf),
             V((2 * rs + 1, D * B, D * B), bf), V((NB, D * B), bf),
             V((C, D * B, NB), bf), V((rs, D * B, NB), bf),
-            V((2, D * B, NB), f32), V((2, Y, Z, share, NB), f32),
-            V((2, Z, share, NB), bf), V((2, Z, share, NB), bf),
-            V((2, Z, share, NB), bf), V((2, share, NB), f32), V((2, Z, share, NB), bf),
-            S((2,)), S((3, C, 2)), S((C, 2)), S((rs, 2)), S((rs, 2)), S((2,)), S((2,)), S((2, Z)), S((2, Z)),
+            V((2, D * B, NB), f32), V((2, N, Y, Z, share, width), f32),
+            V((2, N, Z, share, width), bf), V((2, N, Z, share, width), bf),
+            V((2, N, Z, share, width), bf), V((2, N, share, width), f32), V((2, N, Z, share, width), bf),
+            S((2,)), S((3, C, 4)), S((C, 4)), S((rs, 4)), S((rs, 4)), S((2, N)), S((2, N)), S((2, N, Z)), S((2, N, Z)),
         ],
         compiler_params=pltpu.CompilerParams(collective_id=0, has_side_effects=True,
                                              vmem_limit_bytes=60 * 1024 * 1024),

time: 70.2 us -> 69.6 us (level)
  no operation moved by 1% of the time
where the time goes in v3:
time: 69.6 us; the launch traced here: 69.4 us
  Pallas kernels  65.7 us (94%)
  local copies, waits for them, and re-layouts  2.04 us (3%)
  other arithmetic  1.6 us (2%)
    pallas_call x1, Pallas kernels, local(): pl.pallas_call(functools.partial(kernel, (R, C, Z, Y, D, KA, KP, B, CBR))...  65.7 us
    unnamed x4, local copies, waits for them, and re-layouts  1.87 us

profile of v3, /device:TPU:1, one launch (start us, length us, event | category | flops | bytes accessed | tf_op | source)
XLA Modules:
  0.0 69.4 jit_solution(6324346354171593456)
XLA Ops:
  0.0 0.0 copy-start
  0.0 0.7 %add_select_fusion = s32[4,27]{1,0:T(4,128)S(1)} fusion(s32[4,27]{1,0:T(4,128)} %param.5, s32[]{:T(128)S(6)} %mul.7), kind=kLoop, calls=%fused_computation.4 | loop fusion | flops 1404 | bytes 868 | tf_op jit(solution)/shard_map/jit(remainder)/select_n | solution.py:293
  0.7 0.0 copy-done
  0.7 0.1 constant_dynamic-slice_fusion
  0.8 0.1 copy.8
  0.9 0.1 select_reduce_fusion.1
  1.0 0.1 copy.7
  1.1 0.1 select_reduce_fusion
  1.2 0.7 pad_add_fusion.slots
  1.9 65.7 %shard_map.46 = f32[64,1536]{1,0:T(8,128)} custom-call(s32[4,40]{1,0:T(4,128)} %pad_add_fusion.slots, bf16[4,27,128,128]{3,2,1,0:T(8,128)(2,1)} %a_hbm.1, bf16[4,4,128,128]{3,2,1,0:T(8,128)(2,1)} %p_hbm.1), custom_call_target="tpu_custom_call" | custom-call | tf_op jit(solution)/shard_map/pallas_call | solution.py:304
  67.6 1.8 %copy.10 = f32[64,1536]{1,0:T(8,128)} copy(f32[64,1536]{1,0:T(8,128)} %shard_map.46) | data formatting | bytes 786432
  (5 shorter events, 0.0 us)
Async XLA Ops:
  0.0 0.7 %copy-start = (s32[128,4]{0,1:T(4,128)S(1)}, s32[128,4]{0,1:T(4,128)}, u32[]{:S(2)}) copy-start(s32[128,4]{0,1:T(4,128)} %param.7) | copy-start | bytes 6148
